TPU v7x, 512 devices: a whole 4x4x16 slice. The times are simulated.
512 devices in a mesh: geo: 64 (over z, y), cell: 8 (over x, core).
Axes of the slice: x: 4, y: 4, z: 16, core: 2. Of those that a mesh axis runs over, the one named last changes fastest.
Arguments:
- detail_rows: float32 [8192, 2048], P('geo', 'cell'), may hold values from -60 to 60
- row_block: int32 [8192], P('geo'), may hold values from 0 to 8191, as said below
- block_weight: int32 [8192], P('geo'), may hold values from 1 to 9
- block_group: int32 [8192], P('geo'), may hold values from 0 to 63, as said below
- query_matrix: int32 [2048, 512], P('cell'), may hold values 0 or 1
- query_weight: float32 [512], replicated, may hold values from 0.0048828125 to 0.048828125
- query_noisy: float32 [8192, 512], P('geo'), may hold values from -48 to 48
- group_noisy: float32 [64, 2048], P(None, 'cell'), may hold values from -48 to 48
Outputs:
- solution_field: float32 [8192, 2048], P('geo', 'cell')
- residual: float32 [8192, 2048], P('geo', 'cell')
Inputs may be any that keep to these rules, and one draw needn't show every extreme that they name: row_block is a permutation of all blocks; arrival row r lies on geo index r // 128 and its block lies on geo index (r mod 128) // 2, so each geo index sends 2 rows to each geo index. `block_group`: every group holds exactly 128 blocks.
All inputs are finite; a program needn't handle non-finite values. No bound on the sum of `query_matrix` on one device may be relied on, other than what follows from the above.
Results may differ from a plain program's by a relative error of at most 0.0029.
Values sent between devices are 32-bit elements; how exact they have to be, the bound alone decides.
A program may use at most 64 MiB of HBM per device.

v0:
```python
import jax
import jax.numpy as jnp
from jax import lax
from jax.sharding import PartitionSpec as P

QUERIES = 512
ITERS = 2
BLK_DEV = 128
AGG_WEIGHT = 0.25
HIGHEST_PREC = lax.Precision.HIGHEST
LEADING_DIMS = (((0,), (1,)), ((), ()))


def local(
    detail_rows,
    row_block,
    block_weight,
    block_group,
    query_matrix,
    query_weight,
    query_noisy,
    group_noisy,
):
    geo_index = lax.axis_index("geo")
    sent_ids = row_block.astype(jnp.float32)
    rows_in, ids_in = (
        lax.all_to_all(detail_rows, "geo", split_axis=0, concat_axis=0, tiled=True),
        lax.all_to_all(sent_ids, "geo", split_axis=0, concat_axis=0, tiled=True),
    )
    local_rows = ids_in.astype(jnp.int32) - geo_index * BLK_DEV
    detail = jnp.zeros(detail_rows.shape, jnp.float32).at[local_rows].set(rows_in)
    weight = block_weight.astype(jnp.float32)[:, None]
    queries = query_matrix.astype(jnp.float32)
    group_count = group_noisy.shape[0]
    share_rows = QUERIES // lax.axis_size("cell")

    def squares(vector):
        return lax.psum(jnp.sum(vector * vector), ("geo", "cell"))

    right_side = weight * detail
    right_side = right_side + jnp.dot(
        query_noisy * query_weight[None, :],
        queries.T,
        precision=HIGHEST_PREC,
        preferred_element_type=jnp.float32,
    )
    right_side = right_side + AGG_WEIGHT * group_noisy[block_group]
    solution_field = jnp.zeros_like(right_side)
    residual = right_side
    direction = right_side
    norm_now = squares(residual)
    for iteration in range(ITERS):
        partial_totals = jax.ops.segment_sum(direction, block_group, num_segments=group_count)
        totals = lax.psum(partial_totals, "geo")
        estimate = direction
        share_part = lax.psum_scatter(
            lax.dot_general(
                queries,
                estimate,
                LEADING_DIMS,
                precision=HIGHEST_PREC,
                preferred_element_type=jnp.float32,
            ),
            "cell",
            scatter_dimension=0,
            tiled=True,
        )
        scales = lax.dynamic_slice_in_dim(
            query_weight, lax.axis_index("cell") * share_rows, share_rows, 0
        )
        share_part = share_part * scales[:, None]
        spread_back = lax.dot_general(
            lax.all_gather(share_part, "cell", axis=0, tiled=True),
            queries,
            LEADING_DIMS,
            precision=HIGHEST_PREC,
            preferred_element_type=jnp.float32,
        )
        image_vec = weight * direction + spread_back + AGG_WEIGHT * totals[block_group]
        step_size = norm_now / lax.psum(jnp.sum(direction * image_vec), ("geo", "cell"))
        solution_field = solution_field + step_size * direction
        residual = residual - step_size * image_vec
        norm_next = squares(residual)
        direction = residual + norm_next / norm_now * direction
        norm_now = norm_next
    return (solution_field, residual)


def solution(mesh):
    return jax.shard_map(
        local,
        mesh=mesh,
        in_specs=(
            P("geo", "cell"),
            P("geo"),
            P("geo"),
            P("geo"),
            P("cell", None),
            P(),
            P("geo", None),
            P(None, "cell"),
        ),
        out_specs=(P("geo", "cell"), P("geo", "cell")),
        check_vma=False,
    )
```

profile of v0, /device:TPU:1, one launch (start us, length us, event | category | flops | bytes accessed | tf_op | source)
XLA Modules:
  0.0 915.7 jit_solution(15356650263555236824)
XLA Ops:
  8.7 0.8 all_to_all.14
  9.5 19.3 %all-to-all-start = ((f32[64,2,1]{1,2,0:T(1,128)}), f32[64,2,1]{1,2,0:T(1,128)S(1)}, u32[]{:S(2)}, u32[]{:S(2)}) async-start(f32[64,2,1]{1,2,0:T(1,128)} %bitcast), calls=%async_computation | async-start | bytes 65536 | tf_op jit(solution)/shard_map/all_to_all | solution.py:28
  28.7 1.6 all_to_all.16
  30.4 11.7 %all-to-all-done = f32[64,2,1]{1,2,0:T(1,128)S(1)} async-done(((f32[64,2,1]{1,2,0:T(1,128)}), f32[64,2,1]{1,2,0:T(1,128)S(1)}, u32[]{:S(2)}, u32[]{:S(2)}) %all-to-all-start) | async-done | bytes 544 | tf_op jit(solution)/shard_map/all_to_all | solution.py:28
  42.1 4.6 all-to-all-start.1
  48.6 13.3 %all-to-all-done.1 = f32[64,2,256]{2,1,0:T(2,128)S(1)} async-done(((f32[64,2,256]{2,1,0:T(2,128)}), f32[64,2,256]{2,1,0:T(2,128)S(1)}, u32[]{:S(2)}, u32[]{:S(2)}) %all-to-all-start.1) | async-done | bytes 131104 | tf_op jit(solution)/shard_map/all_to_all | solution.py:27
  62.0 1.0 scatter_custom_fusion
  63.8 1.8 scatter_custom_fusion.1
  66.1 0.8 copy.16
  67.1 238.7 %all-reduce.4.cloned.1.call-done = f32[64,256]{1,0:T(8,128)} async-done(((f32[64,256]{1,0:T(8,128)}), f32[64,256]{1,0:T(8,128)}) %all-reduce.4.cloned.1.call-update) | async-done | bytes 65552 | tf_op jit(solution)/shard_map/psum | solution.py:54
  305.8 1.6 gather_fusion.1
  307.4 0.8 broadcast_multiply_fusion.1
  308.3 23.9 %all_gather.6 = f32[512,128]{1,0:T(8,128)S(1)} all-gather(f32[64,128]{1,0:T(8,128)S(1)} %broadcast_multiply_fusion.1), channel_id=1, replica_groups=mesh['geo'=64,'cell'=8] {'cell'}, dimensions={0}, use_global_device_ids=true | all-gather | bytes 294912 | tf_op jit(solution)/shard_map/all_gather | solution.py:73
  332.2 1.2 multiply_reduce_fusion.2
  333.4 100.5 %all-reduce = (f32[]{:T(128)}, f32[]{:T(128)}) all-reduce(f32[]{:T(128)} %get-tuple-element.3, f32[]{:T(128)} %get-tuple-element.2), channel_id=1, replica_groups=mesh['geo'=64,'cell'=8] {'geo','cell'}, use_global_device_ids=true, to_apply=%region_2.0 | all-reduce | flops 2 | bytes 16 | tf_op jit(solution)/shard_map/psum | solution.py:38
  435.8 99.4 %psum.45 = f32[]{:T(128)} all-reduce(f32[]{:T(128)} %multiply_reduce_fusion.1), channel_id=1, replica_groups=mesh['geo'=64,'cell'=8] {'geo','cell'}, use_global_device_ids=true, to_apply=%region_9.0 | all-reduce | flops 1 | bytes 8 | tf_op jit(solution)/shard_map/psum | solution.py:38
  536.6 1.8 scatter_custom_fusion.2
  538.9 0.8 copy.18
  539.8 238.5 %all-reduce.6.cloned.1.call-done = f32[64,256]{1,0:T(8,128)} async-done(((f32[64,256]{1,0:T(8,128)}), f32[64,256]{1,0:T(8,128)}) %all-reduce.6.cloned.1.call-update) | async-done | bytes 65552 | tf_op jit(solution)/shard_map/psum | solution.py:54
  778.3 1.6 gather_fusion.2
  779.9 0.8 broadcast_multiply_fusion
  780.7 23.9 %all_gather.7 = f32[512,128]{1,0:T(8,128)S(1)} all-gather(f32[64,128]{1,0:T(8,128)S(1)} %broadcast_multiply_fusion), channel_id=1, replica_groups=mesh['geo'=64,'cell'=8] {'cell'}, dimensions={0}, use_global_device_ids=true | all-gather | bytes 294912 | tf_op jit(solution)/shard_map/all_gather | solution.py:73
  804.6 1.2 multiply_reduce_fusion
  805.8 100.4 %psum.47 = f32[]{:T(128)} all-reduce(f32[]{:T(128)} %get-tuple-element.9), channel_id=1, replica_groups=mesh['geo'=64,'cell'=8] {'geo','cell'}, use_global_device_ids=true, to_apply=%region_14.0 | all-reduce | flops 1 | bytes 8 | tf_op jit(solution)/shard_map/psum | solution.py:80
  (38 shorter events, 5.8 us)
Async XLA Ops:
  8.0 39.5 %copy-start = (f32[64,256]{1,0:T(8,128)S(1)}, f32[64,256]{1,0:T(8,128)}, u32[]{:S(2)}) copy-start(f32[64,256]{1,0:T(8,128)} %param.15) | copy-start | bytes 196612
  9.5 32.7 %all-to-all-start = ((f32[64,2,1]{1,2,0:T(1,128)}), f32[64,2,1]{1,2,0:T(1,128)S(1)}, u32[]{:S(2)}, u32[]{:S(2)}) async-start(f32[64,2,1]{1,2,0:T(1,128)} %bitcast), calls=%async_computation | async-start | bytes 65536 | tf_op jit(solution)/shard_map/all_to_all | solution.py:28
  30.4 16.4 %copy-start.5 = (s32[128]{0:T(128)S(1)}, s32[128]{0:T(128)}, u32[]{:S(2)}) copy-start(s32[128]{0:T(128)} %param.11) | copy-start | bytes 1540
  42.1 19.8 %all-to-all-start.1 = ((f32[64,2,256]{2,1,0:T(2,128)}), f32[64,2,256]{2,1,0:T(2,128)S(1)}, u32[]{:S(2)}, u32[]{:S(2)}) async-start(f32[64,2,256]{2,1,0:T(2,128)} %all_to_all.16), calls=%async_computation.1 | async-start | bytes 262144 | tf_op jit(solution)/shard_map/all_to_all | solution.py:27
  46.8 259.0 %all-reduce.4.cloned.1.call-start = ((), (), s32[]{:S(2)}) async-start(), calls=%async_computation.4 | async-start | bytes 131072 | tf_op jit(solution)/shard_map/psum | solution.py:54
  46.8 0.7 copy-start.4
  47.5 15.6 %copy-start.1 = (s32[256,512]{1,0:T(8,128)S(1)}, s32[256,512]{1,0:T(8,128)}, u32[]{:S(2)}) copy-start(s32[256,512]{1,0:T(8,128)} %param.12) | copy-start | bytes 1572868
  48.3 14.8 %copy-start.2 = (f32[128,512]{1,0:T(8,128)S(1)}, f32[128,512]{1,0:T(8,128)}, u32[]{:S(2)}) copy-start(f32[128,512]{1,0:T(8,128)} %param.14) | copy-start | bytes 786436
  62.0 1.1 copy-start.3
  65.6 241.8 %reduce-scatter.7.cloned.1.call-start = ((), (), s32[]{:S(2)}) async-start(), calls=%async_computation.6 | async-start | bytes 294912 | tf_op jit(solution)/shard_map/reduce_scatter | solution.py:56
  67.0 711.3 %all-reduce.6.cloned.1.call-start = ((), (), s32[]{:S(2)}) async-start(), calls=%async_computation.5 | async-start | bytes 131072 | tf_op jit(solution)/shard_map/psum | solution.py:54
  538.4 241.5 %reduce-scatter.9.cloned.1.call-start = ((), (), s32[]{:S(2)}) async-start(), calls=%async_computation.7 | async-start | bytes 294912 | tf_op jit(solution)/shard_map/reduce_scatter | solution.py:56
Sparse Core Ops, SparseCore 0:
  65.8 239.9 all-reduce.3
  538.5 239.6 all-reduce.5
Sparse Core Ops, SparseCore 1:
  68.9 29.8 reduce-scatter.6
  541.9 28.9 reduce-scatter.8
where the time goes:
time: 917 us; the launch traced here: 916 us
  waiting for transfers between devices  502 us (55%)
  blocking collectives  348 us (38%)
  starting transfers between devices  24.1 us (3%)
  between operations  19.7 us (2%)
  local copies, waits for them, and re-layouts  10 us (1%)
    psum x2, waiting for transfers between devices, local(): totals = lax.psum(partial_totals, 'geo')  477 us
    psum x2, blocking collectives, squares(): return lax.psum(jnp.sum(vector * vector), ('geo', 'cell'))  200 us
    psum x1, blocking collectives, local(): lax.psum(jnp.sum(direction * image_vec), ('geo', 'cell'))  100 us
    all_gather x2, blocking collectives, local(): lax.all_gather(share_part, 'cell', axis=0, tiled=True)  47.8 us
    all_to_all x1, starting transfers between devices, local(): lax.all_to_all(sent_ids, 'geo', split_axis=0, concat_axis=0, tiled=True)  19.3 us
  transfers between devices with their start and end apart: 6, of which 4 were waited for; matrix products, arithmetic and copies ran while one was open for 1% of the time, Pallas kernels for 0%

commit v1 on v0

--- a/solution.py
+++ b/solution.py
@@ -9,6 +9,28 @@
 AGG_WEIGHT = 0.25
 HIGHEST_PREC = lax.Precision.HIGHEST
 LEADING_DIMS = (((0,), (1,)), ((), ()))
+
+
+def joined_along(blocks, dim):
+    shape = list(blocks.shape[1:])
+    shape[dim] *= blocks.shape[0]
+    return jnp.moveaxis(blocks, 0, dim).reshape(shape)
+
+
+def collect(x, axis, dim):
+    peers = lax.axis_size(axis)
+    pairs = [(i, (i + 1) % peers) for i in range(peers)]
+    back = [(b, a) for a, b in pairs]
+    lower, upper = ([], [])
+    for step in range(peers - 1):
+        if step % 2 == 0:
+            lower.append(lax.ppermute(lower[-1] if lower else x, axis, pairs))
+        else:
+            upper.append(lax.ppermute(upper[-1] if upper else x, axis, back))
+    tiles = jnp.stack([*lower[::-1], x, *upper])
+    shift = lax.axis_index(axis) - len(lower)
+    tiles = tiles[(jnp.arange(peers) - shift) % peers]
+    return joined_along(tiles, dim)
 
 
 def local(
@@ -70,7 +92,7 @@
         )
         share_part = share_part * scales[:, None]
         spread_back = lax.dot_general(
-            lax.all_gather(share_part, "cell", axis=0, tiled=True),
+            collect(share_part, "cell", 0),
             queries,
             LEADING_DIMS,
             precision=HIGHEST_PREC,

time: 917 us -> 991 us (1.081)
  waiting for transfers between devices: 502 us -> 584 us
  blocking collectives: 348 us -> 299 us
  starting transfers between devices: 24.1 us -> 63.8 us
    reduce_scatter x2, waiting for transfers between devices: 0.05 us -> 58.2 us  [local(): lax.psum_scatter(lax.dot_general(queries, estimate, LEADING_DIMS, precisi...]
    all_gather x2 -> x0, blocking collectives: 47.8 us -> none  [local(): lax.all_gather(share_part, 'cell', axis=0, tiled=True)]
    ppermute x0 -> x14, starting transfers between devices: none -> 39.7 us  [the longest x6 37.6 us: collect(): upper.append(lax.ppermute(upper[-1] if upper else x, axis, back))]
    psum x2, waiting for transfers between devices: 477 us -> 490 us  [local(): totals = lax.psum(partial_totals, 'geo')]
    ppermute x0 -> x14, waiting for transfers between devices: none -> 10.4 us  [the longest x8 5.93 us: collect(): lower.append(lax.ppermute(lower[-1] if lower else x, axis, pairs))]
  transfers between devices with their start and end apart: 6 -> 20, of which waited for: 4 -> 12; matrix products, arithmetic and copies ran while one was open for 1% -> 1% of each run, Pallas kernels for 0% -> 0%
where the time goes in v1:
time: 991 us; the launch traced here: 990 us
  waiting for transfers between devices  584 us (59%)
  blocking collectives  299 us (30%)
  starting transfers between devices  63.8 us (6%)
  between operations  19.6 us (2%)
  local copies, waits for them, and re-layouts  12.7 us (1%)
    psum x2, waiting for transfers between devices, local(): totals = lax.psum(partial_totals, 'geo')  490 us
    psum x2, blocking collectives, squares(): return lax.psum(jnp.sum(vector * vector), ('geo', 'cell'))  199 us
    psum x1, blocking collectives, local(): lax.psum(jnp.sum(direction * image_vec), ('geo', 'cell'))  99.7 us
    reduce_scatter x2, waiting for transfers between devices, local(): lax.psum_scatter(lax.dot_general(queries, estimate, LEADING_DIMS, precisi...  58.2 us
    ppermute x6, starting transfers between devices, collect(): upper.append(lax.ppermute(upper[-1] if upper else x, axis, back))  37.6 us
  transfers between devices with their start and end apart: 20, of which 12 were waited for; matrix products, arithmetic and copies ran while one was open for 1% of the time, Pallas kernels for 0%

profile of v1, /device:TPU:1, one launch (start us, length us, event | category | flops | bytes accessed | tf_op | source)
XLA Modules:
  0.0 990.5 jit_solution(12859310589501012251)
XLA Ops:
  9.5 19.3 %all-to-all-start = ((f32[64,2,1]{1,2,0:T(1,128)}), f32[64,2,1]{1,2,0:T(1,128)S(1)}, u32[]{:S(2)}, u32[]{:S(2)}) async-start(f32[64,2,1]{1,2,0:T(1,128)} %bitcast), calls=%async_computation | async-start | bytes 65536 | tf_op jit(solution)/shard_map/all_to_all | solution.py:50
  28.7 1.6 all_to_all.16
  30.4 11.7 %all-to-all-done = f32[64,2,1]{1,2,0:T(1,128)S(1)} async-done(((f32[64,2,1]{1,2,0:T(1,128)}), f32[64,2,1]{1,2,0:T(1,128)S(1)}, u32[]{:S(2)}, u32[]{:S(2)}) %all-to-all-start) | async-done | bytes 544 | tf_op jit(solution)/shard_map/all_to_all | solution.py:50
  42.1 4.6 all-to-all-start.1
  48.6 13.3 %all-to-all-done.1 = f32[64,2,256]{2,1,0:T(2,128)S(1)} async-done(((f32[64,2,256]{2,1,0:T(2,128)}), f32[64,2,256]{2,1,0:T(2,128)S(1)}, u32[]{:S(2)}, u32[]{:S(2)}) %all-to-all-start.1) | async-done | bytes 131104 | tf_op jit(solution)/shard_map/all_to_all | solution.py:49
  65.2 29.3 %reduce-scatter.7.cloned.1.call-done = f32[64,128]{1,0:T(8,128)} async-done(((f32[512,128]{1,0:T(8,128)}), f32[64,128]{1,0:T(8,128)}) %reduce-scatter.7.cloned.1.call-update) | async-done | bytes 32784 | tf_op jit(solution)/shard_map/reduce_scatter | solution.py:78
  95.6 2.6 collective-permute-done
  99.0 3.1 collective-permute-start.4
  102.8 1.8 scatter_custom_fusion.1
  104.7 3.9 collective-permute-start.5
  108.6 247.2 %all-reduce.4.cloned.1.call-done = f32[64,256]{1,0:T(8,128)} async-done(((f32[64,256]{1,0:T(8,128)}), f32[64,256]{1,0:T(8,128)}) %all-reduce.4.cloned.1.call-update) | async-done | bytes 65552 | tf_op jit(solution)/shard_map/psum | solution.py:76
  357.4 11.9 %collective-permute-start.6 = (f32[64,128]{1,0:T(8,128)S(1)}, f32[64,128]{1,0:T(8,128)S(1)}, u32[]{:S(2)}, u32[]{:S(2)}) collective-permute-start(f32[64,128]{1,0:T(8,128)S(1)} %collective-permute-done.5), channel_id=1, source_target_pairs={{1,0},{2,1},{3,2},{4,3},{5,4},{6,5},{7,6},{0,7},{9,8},{10,9},{11,1... | collective-permute-start | bytes 98312 | tf_op jit(solution)/shard_map/ppermute | solution.py:29
  370.2 1.8 collective-permute-done.6
  373.8 99.8 %all-reduce = (f32[]{:T(128)}, f32[]{:T(128)}) all-reduce(f32[]{:T(128)} %get-tuple-element.3, f32[]{:T(128)} %get-tuple-element.2), channel_id=1, replica_groups=mesh['geo'=64,'cell'=8] {'geo','cell'}, use_global_device_ids=true, to_apply=%region_2.0 | all-reduce | flops 2 | bytes 16 | tf_op jit(solution)/shard_map/psum | solution.py:60
  475.6 99.4 %psum.45 = f32[]{:T(128)} all-reduce(f32[]{:T(128)} %multiply_reduce_fusion.1), channel_id=1, replica_groups=mesh['geo'=64,'cell'=8] {'geo','cell'}, use_global_device_ids=true, to_apply=%region_9.10 | all-reduce | flops 1 | bytes 8 | tf_op jit(solution)/shard_map/psum | solution.py:60
  577.6 29.0 %reduce-scatter.9.cloned.1.call-done = f32[64,128]{1,0:T(8,128)} async-done(((f32[512,128]{1,0:T(8,128)}), f32[64,128]{1,0:T(8,128)}) %reduce-scatter.9.cloned.1.call-update) | async-done | bytes 32784 | tf_op jit(solution)/shard_map/reduce_scatter | solution.py:78
  607.7 2.6 collective-permute-done.7
  611.0 1.8 scatter_custom_fusion.2
  612.9 3.1 collective-permute-start.11
  616.9 3.7 collective-permute-start.12
  620.6 242.8 %all-reduce.6.cloned.1.call-done = f32[64,256]{1,0:T(8,128)} async-done(((f32[64,256]{1,0:T(8,128)}), f32[64,256]{1,0:T(8,128)}) %all-reduce.6.cloned.1.call-update) | async-done | bytes 65552 | tf_op jit(solution)/shard_map/psum | solution.py:76
  865.0 11.9 %collective-permute-start.13 = (f32[64,128]{1,0:T(8,128)S(1)}, f32[64,128]{1,0:T(8,128)S(1)}, u32[]{:S(2)}, u32[]{:S(2)}) collective-permute-start(f32[64,128]{1,0:T(8,128)S(1)} %collective-permute-done.12), channel_id=1, source_target_pairs={{1,0},{2,1},{3,2},{4,3},{5,4},{6,5},{7,6},{0,7},{9,8},{10,9},{11,1... | collective-permute-start | bytes 98312 | tf_op jit(solution)/shard_map/ppermute | solution.py:29
  877.8 1.8 collective-permute-done.13
  881.3 99.7 %psum.47 = f32[]{:T(128)} all-reduce(f32[]{:T(128)} %get-tuple-element.9), channel_id=1, replica_groups=mesh['geo'=64,'cell'=8] {'geo','cell'}, use_global_device_ids=true, to_apply=%region_14.15 | all-reduce | flops 1 | bytes 8 | tf_op jit(solution)/shard_map/psum | solution.py:102
  (88 shorter events, 22.9 us)
Async XLA Ops:
  8.0 39.5 %copy-start = (f32[64,256]{1,0:T(8,128)S(1)}, f32[64,256]{1,0:T(8,128)}, u32[]{:S(2)}) copy-start(f32[64,256]{1,0:T(8,128)} %param.15) | copy-start | bytes 196612
  9.5 32.7 %all-to-all-start = ((f32[64,2,1]{1,2,0:T(1,128)}), f32[64,2,1]{1,2,0:T(1,128)S(1)}, u32[]{:S(2)}, u32[]{:S(2)}) async-start(f32[64,2,1]{1,2,0:T(1,128)} %bitcast), calls=%async_computation | async-start | bytes 65536 | tf_op jit(solution)/shard_map/all_to_all | solution.py:50
  30.4 16.4 %copy-start.7 = (s32[128]{0:T(128)S(1)}, s32[128]{0:T(128)}, u32[]{:S(2)}) copy-start(s32[128]{0:T(128)} %param.11) | copy-start | bytes 1540
  42.1 19.8 %all-to-all-start.1 = ((f32[64,2,256]{2,1,0:T(2,128)}), f32[64,2,256]{2,1,0:T(2,128)S(1)}, u32[]{:S(2)}, u32[]{:S(2)}) async-start(f32[64,2,256]{2,1,0:T(2,128)} %all_to_all.16), calls=%async_computation.1 | async-start | bytes 262144 | tf_op jit(solution)/shard_map/all_to_all | solution.py:49
  46.8 47.7 %reduce-scatter.7.cloned.1.call-start = ((), (), s32[]{:S(2)}) async-start(), calls=%async_computation.6 | async-start | bytes 294912 | tf_op jit(solution)/shard_map/reduce_scatter | solution.py:78
  47.5 15.6 %copy-start.1 = (s32[256,512]{1,0:T(8,128)S(1)}, s32[256,512]{1,0:T(8,128)}, u32[]{:S(2)}) copy-start(s32[256,512]{1,0:T(8,128)} %param.12) | copy-start | bytes 1572868
  48.3 14.8 %copy-start.2 = (f32[128,512]{1,0:T(8,128)S(1)}, f32[128,512]{1,0:T(8,128)}, u32[]{:S(2)}) copy-start(f32[128,512]{1,0:T(8,128)} %param.14) | copy-start | bytes 786436
  65.1 290.7 %all-reduce.4.cloned.1.call-start = ((), (), s32[]{:S(2)}) async-start(), calls=%async_computation.4 | async-start | bytes 131072 | tf_op jit(solution)/shard_map/psum | solution.py:76
  95.3 2.9 collective-permute-start
  98.2 4.6 collective-permute-start.1
  99.0 5.7 collective-permute-start.4
  102.8 5.8 collective-permute-start.2
  104.7 501.9 %reduce-scatter.9.cloned.1.call-start = ((), (), s32[]{:S(2)}) async-start(), calls=%async_computation.7 | async-start | bytes 294912 | tf_op jit(solution)/shard_map/reduce_scatter | solution.py:78
  104.7 252.7 %collective-permute-start.5 = (f32[64,128]{1,0:T(8,128)S(1)}, f32[64,128]{1,0:T(8,128)S(1)}, u32[]{:S(2)}, u32[]{:S(2)}) collective-permute-start(f32[64,128]{1,0:T(8,128)S(1)} %collective-permute-done.4), channel_id=1, source_target_pairs={{1,0},{2,1},{3,2},{4,3},{5,4},{6,5},{7,6},{0,7},{9,8},{10,9},{11,1... | collective-permute-start | bytes 98312 | tf_op jit(solution)/shard_map/ppermute | solution.py:29
  108.6 260.7 %collective-permute-start.3 = (f32[64,128]{1,0:T(8,128)S(1)}, f32[64,128]{1,0:T(8,128)S(1)}, u32[]{:S(2)}, u32[]{:S(2)}) collective-permute-start(f32[64,128]{1,0:T(8,128)S(1)} %collective-permute-done.2), channel_id=1, source_target_pairs={{0,1},{1,2},{2,3},{3,4},{4,5},{5,6},{6,7},{7,0},{8,9},{9,10},{10,1... | collective-permute-start | bytes 98312 | tf_op jit(solution)/shard_map/ppermute | solution.py:27
  357.4 14.6 %collective-permute-start.6 = (f32[64,128]{1,0:T(8,128)S(1)}, f32[64,128]{1,0:T(8,128)S(1)}, u32[]{:S(2)}, u32[]{:S(2)}) collective-permute-start(f32[64,128]{1,0:T(8,128)S(1)} %collective-permute-done.5), channel_id=1, source_target_pairs={{1,0},{2,1},{3,2},{4,3},{5,4},{6,5},{7,6},{0,7},{9,8},{10,9},{11,1... | collective-permute-start | bytes 98312 | tf_op jit(solution)/shard_map/ppermute | solution.py:29
  577.5 285.8 %all-reduce.6.cloned.1.call-start = ((), (), s32[]{:S(2)}) async-start(), calls=%async_computation.5 | async-start | bytes 131072 | tf_op jit(solution)/shard_map/psum | solution.py:76
  607.4 2.9 collective-permute-start.7
  610.3 5.7 collective-permute-start.8
  612.9 4.0 collective-permute-start.11
  616.0 4.6 collective-permute-start.9
  616.9 248.1 %collective-permute-start.12 = (f32[64,128]{1,0:T(8,128)S(1)}, f32[64,128]{1,0:T(8,128)S(1)}, u32[]{:S(2)}, u32[]{:S(2)}) collective-permute-start(f32[64,128]{1,0:T(8,128)S(1)} %collective-permute-done.11), channel_id=1, source_target_pairs={{1,0},{2,1},{3,2},{4,3},{5,4},{6,5},{7,6},{0,7},{9,8},{10,9},{11,1... | collective-permute-start | bytes 98312 | tf_op jit(solution)/shard_map/ppermute | solution.py:29
  620.6 256.3 %collective-permute-start.10 = (f32[64,128]{1,0:T(8,128)S(1)}, f32[64,128]{1,0:T(8,128)S(1)}, u32[]{:S(2)}, u32[]{:S(2)}) collective-permute-start(f32[64,128]{1,0:T(8,128)S(1)} %collective-permute-done.9), channel_id=1, source_target_pairs={{0,1},{1,2},{2,3},{3,4},{4,5},{5,6},{6,7},{7,0},{8,9},{9,10},{10,1... | collective-permute-start | bytes 98312 | tf_op jit(solution)/shard_map/ppermute | solution.py:27
  865.0 14.6 %collective-permute-start.13 = (f32[64,128]{1,0:T(8,128)S(1)}, f32[64,128]{1,0:T(8,128)S(1)}, u32[]{:S(2)}, u32[]{:S(2)}) collective-permute-start(f32[64,128]{1,0:T(8,128)S(1)} %collective-permute-done.12), channel_id=1, source_target_pairs={{1,0},{2,1},{3,2},{4,3},{5,4},{6,5},{7,6},{0,7},{9,8},{10,9},{11,1... | collective-permute-start | bytes 98312 | tf_op jit(solution)/shard_map/ppermute | solution.py:29
  (4 other events, 3.3 us)
Sparse Core Ops, SparseCore 0:
  65.2 29.2 reduce-scatter.6
  577.7 28.8 reduce-scatter.8
Sparse Core Ops, SparseCore 1:
  104.8 251.0 all-reduce.3
  613.0 250.3 all-reduce.5
